TPU v7x, 128 devices: a whole 4x4x4 slice. The times are simulated.
128 devices in a mesh: expert: 32 (over x, z, y_lo), zero: 4 (over y_hi, core).
Axes of the slice: x: 4, y: 4 (y_hi: 2, y_lo: 2; y = y_hi * 2 + y_lo), z: 4, core: 2. Of those that a mesh axis runs over, the one named last changes fastest.
Arguments:
- tokens: bfloat16 [24576, 4096], P(('expert', 'zero')), may hold values from -6 to 6
- expert_ids: int32 [24576, 8], P(('expert', 'zero')), may hold values from 0 to 127, all different within a row; in each aligned block of 192 rows (0 to 191, 192 to 383, ...) at most 24 rows name the same one
- route_weights: bfloat16 [24576, 8], P(('expert', 'zero')), may hold values from 0.049804688 to 0.5
- master_gu: float32 [32, 4096, 1536], P('expert', 'zero'), may hold values from -0.09375 to 0.09375
- grad_gu: bfloat16 [32, 4096, 1536], P('expert', 'zero'), may hold values from -0.015625 to 0.015625
- first_gu: bfloat16 [32, 4096, 1536], P('expert', 'zero'), may hold values from -0.015625 to 0.015625
- second_gu: bfloat16 [32, 4096, 1536], P('expert', 'zero'), may hold values from 9.9651515e-08 to 9.953976e-06
- master_down: float32 [32, 4096, 768], P('expert', 'zero'), may hold values from -0.21875 to 0.21875
- grad_down: bfloat16 [32, 4096, 768], P('expert', 'zero'), may hold values from -0.015625 to 0.015625
- first_down: bfloat16 [32, 4096, 768], P('expert', 'zero'), may hold values from -0.015625 to 0.015625
- second_down: bfloat16 [32, 4096, 768], P('expert', 'zero'), may hold values from 9.9651515e-08 to 9.953976e-06
Outputs:
- mixed: bfloat16 [24576, 4096], P(('expert', 'zero'))
Inputs may be any that keep to these rules, and one draw needn't show every extreme that they name: `expert_ids`: each row names 8 different experts; within the 192 rows of one device no expert is named more than 24 times, a bound that some block reaches.
All inputs are finite; a program needn't handle non-finite values.
Results may differ from a plain program's by a relative error of at most 0.003.
The roundings to bfloat16 on the way count: a program that leaves them out, or rounds other values in their place, can miss the bound.
Values may be sent and summed in bfloat16 or wider, within the bound.
A program may use at most 256 MiB of HBM per device.

v0:
```python
import jax
import jax.numpy as jnp
from jax import lax
from jax.sharding import PartitionSpec as P

EXPERTS = 128
CAP = 24


beta_one = 0.9
beta_two = 0.999
learn_rate = 0.002
adam_eps = 1e-08
corr_one = 1.0
corr_two = 0.63230457523


def adam_step(master, gradient, moment_one, moment_two):
    grads = gradient.astype(jnp.float32)
    first = beta_one * moment_one.astype(jnp.float32) + (1.0 - beta_one) * grads
    second = beta_two * moment_two.astype(jnp.float32) + (1.0 - beta_two) * grads * grads
    return master - learn_rate * (first / corr_one) / (jnp.sqrt(second / corr_two) + adam_eps)


def block_cast(weights):
    lead = weights.shape[:-2]
    height, breadth = weights.shape[-2:]
    blocks = weights.reshape(lead + (height // 128, 128, breadth // 128, 128))
    largest = jnp.max(jnp.abs(blocks), axis=(-3, -1))
    scales = ((largest + 1e-06) / 448.0).astype(jnp.bfloat16)
    quantized = (blocks / scales.astype(jnp.float32)[..., :, None, :, None]).astype(jnp.bfloat16)
    return (quantized.reshape(weights.shape), scales)


def blocks_per_turn(groups):
    if groups >= 16 and groups % 8 == 0:
        return groups // 8
    return 2


def promoted_in(inputs, quantized, scales):
    count = inputs.shape[0]
    depth, outward = quantized.shape
    groups = depth // 128
    width = blocks_per_turn(groups)
    folded = inputs.reshape(count, groups, 128)
    stacked = quantized.reshape(groups, 128, outward)

    def add_blocks(turn, total):
        first = turn * width
        rows = lax.dynamic_slice_in_dim(folded, first, width, 1)
        weights = lax.dynamic_slice_in_dim(stacked, first, width, 0)
        factors = lax.dynamic_slice_in_dim(scales, first, width, 0)
        pieces = lax.dot_general(
            rows, weights, (((2,), (1,)), ((1,), (0,))), preferred_element_type=jnp.float32
        )
        factor = jnp.repeat(factors.astype(jnp.float32), 128, axis=1)
        return total + jnp.sum(pieces * factor[:, None, :], axis=0)

    start = jnp.zeros((count, outward), jnp.float32)
    return lax.fori_loop(0, groups // width, add_blocks, start)


def promoted_out(hidden, quantized, scales):
    count = hidden.shape[0]
    outward, depth = quantized.shape
    groups = depth // 128
    width = blocks_per_turn(groups)
    folded = hidden.reshape(count, groups, 128)
    stacked = quantized.reshape(outward, groups, 128)

    def add_blocks(turn, total):
        first = turn * width
        rows = lax.dynamic_slice_in_dim(folded, first, width, 1)
        weights = lax.dynamic_slice_in_dim(stacked, first, width, 1)
        factors = lax.dynamic_slice_in_dim(scales, first, width, 1)
        pieces = lax.dot_general(
            rows, weights, (((2,), (2,)), ((1,), (1,))), preferred_element_type=jnp.float32
        )
        factor = jnp.repeat(factors.astype(jnp.float32).T, 128, axis=1)
        return total + jnp.sum(pieces * factor[:, None, :], axis=0)

    start = jnp.zeros((count, outward), jnp.float32)
    return lax.fori_loop(0, groups // width, add_blocks, start)


def shards(
    tokens,
    expert_ids,
    route_weights,
    master_gu,
    grad_gu,
    first_gu,
    second_gu,
    master_down,
    grad_down,
    first_down,
    second_down,
):
    experts_here = lax.axis_size("expert")
    local = EXPERTS // experts_here
    tok_rows, choices = expert_ids.shape
    pair_count = tok_rows * choices
    flat_ids = expert_ids.reshape(pair_count)
    onehot = (flat_ids[:, None] == jnp.arange(EXPERTS, dtype=jnp.int32)[None, :]).astype(
        jnp.bfloat16
    )
    order_index = jnp.arange(pair_count, dtype=jnp.int32)
    earlier = (order_index[None, :] < order_index[:, None]).astype(jnp.bfloat16)
    counted = jnp.dot(earlier, onehot, preferred_element_type=jnp.float32)
    slot_of = jnp.sum(counted * onehot.astype(jnp.float32), axis=1).astype(jnp.int32)
    in_flight = flat_ids % local == 0
    placed = jnp.where(in_flight, flat_ids // local * CAP + slot_of, -1).reshape(tok_rows, choices)
    slot_total = experts_here * CAP
    matches = placed[:, :, None] == jnp.arange(slot_total, dtype=jnp.int32)[None, None, :]
    send_map = jnp.any(matches, axis=1).T.astype(jnp.bfloat16)
    outgoing = jnp.dot(send_map, tokens, preferred_element_type=jnp.float32).astype(jnp.bfloat16)
    outgoing = outgoing.reshape(experts_here, CAP, tokens.shape[1])
    combine = jnp.sum(
        jnp.where(matches, route_weights[:, :, None].astype(jnp.float32), 0.0), axis=1
    ).astype(jnp.bfloat16)
    fresh_gu = adam_step(master_gu[0], grad_gu[0], first_gu[0], second_gu[0])
    fresh_down = adam_step(master_down[0], grad_down[0], first_down[0], second_down[0])
    quant_gate, scale_gate = block_cast(fresh_gu)
    quant_lower, scale_lower = block_cast(fresh_down)
    quant_gate, scale_gate, quant_lower, scale_lower = (
        lax.all_gather(quant_gate, "zero", axis=0, tiled=True),
        lax.all_gather(scale_gate, "zero", axis=0, tiled=True),
        lax.all_gather(quant_lower, "zero", axis=0, tiled=True),
        lax.all_gather(scale_lower, "zero", axis=0, tiled=True),
    )
    arrived = lax.all_to_all(outgoing, "expert", split_axis=0, concat_axis=0, tiled=True)
    quant_gate, scale_gate, quant_lower, scale_lower = (
        quant_gate,
        scale_gate,
        quant_lower,
        scale_lower,
    )
    flat_rows = arrived.reshape(-1, arrived.shape[-1])
    gated = promoted_in(flat_rows, quant_gate, scale_gate)
    half = gated.shape[1] // 2
    hidden = (jax.nn.silu(gated[:, :half]) * gated[:, half:]).astype(jnp.bfloat16)
    output = promoted_out(hidden, quant_lower, scale_lower).astype(jnp.bfloat16)
    returned = lax.all_to_all(
        output.reshape(arrived.shape), "expert", split_axis=0, concat_axis=0, tiled=True
    )
    gathered = returned.reshape(slot_total, returned.shape[-1])
    return jnp.dot(combine, gathered, preferred_element_type=jnp.float32).astype(jnp.bfloat16)


def solution(mesh):
    in_specs = (
        P(("expert", "zero"), None),
        P(("expert", "zero"), None),
        P(("expert", "zero"), None),
        P("expert", "zero", None),
        P("expert", "zero", None),
        P("expert", "zero", None),
        P("expert", "zero", None),
        P("expert", "zero", None),
        P("expert", "zero", None),
        P("expert", "zero", None),
        P("expert", "zero", None),
    )
    out_specs = P(("expert", "zero"), None)
    return jax.shard_map(shards, mesh=mesh, in_specs=in_specs, out_specs=out_specs, check_vma=False)
```

profile of v0, /device:TPU:32, one launch (start us, length us, event | category | flops | bytes accessed | tf_op | source)
XLA Modules:
  0.0 585.3 jit_solution(16520240657525353150)
XLA Ops:
  6.5 4.8 copy.120
  14.1 4.2 copy.147
  18.3 4.6 copy.121
  25.6 4.1 copy.148
  29.7 4.7 copy.122
  37.1 4.1 copy.149
  41.3 6.6 %copy.119 = f32[1,1024,1536]{1,2,0:T(8,128)} copy(f32[1,1024,1536]{2,1,0:T(8,128)} %param.18) | data formatting | bytes 12582912 | tf_op args[3]
  47.9 4.5 copy.146
  52.5 8.0 %abs_reduce_fusion = f32[8,12]{0,1:T(8,128)S(1)} fusion(f32[8,128,12,128]{1,0,3,2:T(8,128)S(1)} %bitcast.193, f32[8,128,12,128]{1,0,3,2:T(8,128)S(1)} %bitcast.191, f32[8,128,12,128]{1,0,3,2:T(8,128)} %bitcast.190, f32[8,128,12,128]{1,0,3,2:T(8,128)} %bitcast.188), kind=kLoop, calls=%fused_computation.41 | loop fusion | flops 18874272 | bytes 25166208 | tf_op jit(solution)/shard_map/reduce_max | solution.py:29
  63.5 9.4 %fusion.25 = bf16[1024,1536]{0,1:T(8,128)(2,1)} fusion(f32[192,8,8,128]{3,2,1,0:T(8,128)S(1)} %bitcast.192, bf16[1,1024,1536]{1,2,0:T(8,128)(2,1)} %copy.122, bf16[1,1024,1536]{1,2,0:T(8,128)(2,1)S(1)} %copy-done.3, bf16[1,1024,1536]{1,2,0:T(8,128)(2,1)S(1)} %copy-done.2, f32[1,1024,1536]{1,2,0:T(8,128)} %copy.119), kind=kLoop, calls=%fused_computation.46 | loop fusion | flops 26738688 | bytes 25165824 | tf_op jit(solution)/shard_map/convert_element_type | solution.py:31
  76.7 4.6 convolution_convert_fusion
  81.3 9.2 %all-to-all-start = ((bf16[32,24,4096]{2,1,0:T(8,128)(2,1)}), bf16[32,24,4096]{2,1,0:T(8,128)(2,1)}, u32[]{:S(2)}, u32[]{:S(2)}) async-start(bf16[32,24,4096]{2,1,0:T(8,128)(2,1)} %bitcast.186), calls=%async_computation | async-start | bytes 12582912 | tf_op jit(solution)/shard_map/all_to_all | solution.py:132
  113.0 4.2 abs_reduce_fusion.1
  119.1 3.7 fusion.45
  123.0 64.0 %all_gather.15 = bf16[32,6]{1,0:T(8,128)(2,1)S(1)} all-gather(bf16[8,6]{1,0:T(8,128)(2,1)S(1)} %copy.135), channel_id=1, replica_groups=mesh['expert'=32,'zero'=4] {'zero'}, dimensions={0}, use_global_device_ids=true | all-gather | bytes 480 | tf_op jit(solution)/shard_map/all_gather | solution.py:130
  187.1 6.7 %all_gather.13 = bf16[32,12]{1,0:T(8,128)(2,1)S(1)} all-gather(bf16[8,12]{1,0:T(8,128)(2,1)S(1)} %multiply_convert_fusion.1), channel_id=1, replica_groups=mesh['expert'=32,'zero'=4] {'zero'}, dimensions={0}, use_global_device_ids=true | all-gather | bytes 960 | tf_op jit(solution)/shard_map/all_gather | solution.py:128
  193.8 7.4 %copy.145 = bf16[96,8,32,128]{3,2,1,0:T(8,128)(2,1)} copy(bf16[96,8,32,128]{3,1,2,0:T(8,128)(2,1)} %bitcast.20) | data formatting | bytes 12582912
  201.2 35.2 %all-gather.3.cloned.1.call-done = bf16[4096,1536]{0,1:T(8,128)(2,1)} async-done(((bf16[1024,1536]{0,1:T(8,128)(2,1)}), bf16[4096,1536]{0,1:T(8,128)(2,1)}) %all-gather.3.cloned.1.call-update) | async-done | bytes 12582928 | tf_op jit(solution)/shard_map/all_gather | solution.py:127
  236.3 17.1 %copy.139 = bf16[4096,1536]{1,0:T(8,128)(2,1)} copy(bf16[4096,1536]{0,1:T(8,128)(2,1)} %all-gather.3.cloned.1.call-done) | data formatting | bytes 25165824
  253.4 123.1 %while.28 = (s32[]{:T(128)}, f32[768,1536]{1,0:T(8,128)}, bf16[768,32,128]{2,1,0:T(8,128)(2,1)}, bf16[32,128,1536]{2,1,0:T(8,128)(2,1)}, bf16[32,12]{1,0:T(8,128...) while((s32[]{:T(128)}, f32[768,1536]{1,0:T(8,128)}, ...), condition=%wide.region_6.7_spmd.clone, body=%wide.region_4.6_spmd.clone.sunk | while | flops 1218576384 | bytes 22905472 | solution.py:61
  255.4 6.6 %multiply_reduce_fusion.4 = f32[768,1536]{1,0:T(8,128)} fusion(f32[4,1536]{1,0:T(4,128)S(1)} %bitcast.204, bf16[32,128,1536]{2,1,0:T(8,128)(2,1)} %get-tuple-element.384, s32[]{:T(128)S(6)} %select_n.66, bf16[768,4,128]{2,1,0:T(4,128)(2,1)S(1)} %constant_dynamic-slice_fusion.3), kind=kOutput, calls=%fused_computation.clone.1 | convolution fusion | flops 1216217088 | bytes 7102468 | tf_op jit(solution)/shard_map/while/body/eval_jaxpr/dot_general | solution.py:54
  262.0 5.6 select_add_fusion.4
  269.5 6.6 %multiply_reduce_fusion.4 = f32[768,1536]{1,0:T(8,128)} fusion(f32[4,1536]{1,0:T(4,128)S(1)} %bitcast.204, bf16[32,128,1536]{2,1,0:T(8,128)(2,1)} %get-tuple-element.384, s32[]{:T(128)S(6)} %select_n.66, bf16[768,4,128]{2,1,0:T(4,128)(2,1)S(1)} %constant_dynamic-slice_fusion.3), kind=kOutput, calls=%fused_computation.clone.1 | convolution fusion | flops 1216217088 | bytes 7102468 | tf_op jit(solution)/shard_map/while/body/eval_jaxpr/dot_general | solution.py:54
  276.1 7.1 %select_add_fusion.4 = f32[768,1536]{1,0:T(8,128)} fusion(f32[768,1536]{1,0:T(8,128)} %multiply_reduce_fusion.4, f32[768,1536]{1,0:T(8,128)} %get-tuple-element.373, pred[]{:T(512)S(6)} %compare.13), kind=kLoop, calls=%fused_computation.1.clone.1 | loop fusion | flops 2359296 | bytes 14155777 | tf_op jit(solution)/shard_map/while/body/eval_jaxpr/add | solution.py:58
  285.1 6.7 %multiply_reduce_fusion.4 = f32[768,1536]{1,0:T(8,128)} fusion(f32[4,1536]{1,0:T(4,128)S(1)} %bitcast.204, bf16[32,128,1536]{2,1,0:T(8,128)(2,1)} %get-tuple-element.384, s32[]{:T(128)S(6)} %select_n.66, bf16[768,4,128]{2,1,0:T(4,128)(2,1)S(1)} %constant_dynamic-slice_fusion.3), kind=kOutput, calls=%fused_computation.clone.1 | convolution fusion | flops 1216217088 | bytes 7102468 | tf_op jit(solution)/shard_map/while/body/eval_jaxpr/dot_general | solution.py:54
  291.8 7.0 %select_add_fusion.4 = f32[768,1536]{1,0:T(8,128)} fusion(f32[768,1536]{1,0:T(8,128)} %multiply_reduce_fusion.4, f32[768,1536]{1,0:T(8,128)} %get-tuple-element.373, pred[]{:T(512)S(6)} %compare.13), kind=kLoop, calls=%fused_computation.1.clone.1 | loop fusion | flops 2359296 | bytes 14155777 | tf_op jit(solution)/shard_map/while/body/eval_jaxpr/add | solution.py:58
  300.7 6.6 %multiply_reduce_fusion.4 = f32[768,1536]{1,0:T(8,128)} fusion(f32[4,1536]{1,0:T(4,128)S(1)} %bitcast.204, bf16[32,128,1536]{2,1,0:T(8,128)(2,1)} %get-tuple-element.384, s32[]{:T(128)S(6)} %select_n.66, bf16[768,4,128]{2,1,0:T(4,128)(2,1)S(1)} %constant_dynamic-slice_fusion.3), kind=kOutput, calls=%fused_computation.clone.1 | convolution fusion | flops 1216217088 | bytes 7102468 | tf_op jit(solution)/shard_map/while/body/eval_jaxpr/dot_general | solution.py:54
  307.3 7.0 %select_add_fusion.4 = f32[768,1536]{1,0:T(8,128)} fusion(f32[768,1536]{1,0:T(8,128)} %multiply_reduce_fusion.4, f32[768,1536]{1,0:T(8,128)} %get-tuple-element.373, pred[]{:T(512)S(6)} %compare.13), kind=kLoop, calls=%fused_computation.1.clone.1 | loop fusion | flops 2359296 | bytes 14155777 | tf_op jit(solution)/shard_map/while/body/eval_jaxpr/add | solution.py:58
  316.2 6.6 %multiply_reduce_fusion.4 = f32[768,1536]{1,0:T(8,128)} fusion(f32[4,1536]{1,0:T(4,128)S(1)} %bitcast.204, bf16[32,128,1536]{2,1,0:T(8,128)(2,1)} %get-tuple-element.384, s32[]{:T(128)S(6)} %select_n.66, bf16[768,4,128]{2,1,0:T(4,128)(2,1)S(1)} %constant_dynamic-slice_fusion.3), kind=kOutput, calls=%fused_computation.clone.1 | convolution fusion | flops 1216217088 | bytes 7102468 | tf_op jit(solution)/shard_map/while/body/eval_jaxpr/dot_general | solution.py:54
  322.9 7.0 %select_add_fusion.4 = f32[768,1536]{1,0:T(8,128)} fusion(f32[768,1536]{1,0:T(8,128)} %multiply_reduce_fusion.4, f32[768,1536]{1,0:T(8,128)} %get-tuple-element.373, pred[]{:T(512)S(6)} %compare.13), kind=kLoop, calls=%fused_computation.1.clone.1 | loop fusion | flops 2359296 | bytes 14155777 | tf_op jit(solution)/shard_map/while/body/eval_jaxpr/add | solution.py:58
  331.8 6.6 %multiply_reduce_fusion.4 = f32[768,1536]{1,0:T(8,128)} fusion(f32[4,1536]{1,0:T(4,128)S(1)} %bitcast.204, bf16[32,128,1536]{2,1,0:T(8,128)(2,1)} %get-tuple-element.384, s32[]{:T(128)S(6)} %select_n.66, bf16[768,4,128]{2,1,0:T(4,128)(2,1)S(1)} %constant_dynamic-slice_fusion.3), kind=kOutput, calls=%fused_computation.clone.1 | convolution fusion | flops 1216217088 | bytes 7102468 | tf_op jit(solution)/shard_map/while/body/eval_jaxpr/dot_general | solution.py:54
  338.4 7.0 %select_add_fusion.4 = f32[768,1536]{1,0:T(8,128)} fusion(f32[768,1536]{1,0:T(8,128)} %multiply_reduce_fusion.4, f32[768,1536]{1,0:T(8,128)} %get-tuple-element.373, pred[]{:T(512)S(6)} %compare.13), kind=kLoop, calls=%fused_computation.1.clone.1 | loop fusion | flops 2359296 | bytes 14155777 | tf_op jit(solution)/shard_map/while/body/eval_jaxpr/add | solution.py:58
  347.4 6.6 %multiply_reduce_fusion.4 = f32[768,1536]{1,0:T(8,128)} fusion(f32[4,1536]{1,0:T(4,128)S(1)} %bitcast.204, bf16[32,128,1536]{2,1,0:T(8,128)(2,1)} %get-tuple-element.384, s32[]{:T(128)S(6)} %select_n.66, bf16[768,4,128]{2,1,0:T(4,128)(2,1)S(1)} %constant_dynamic-slice_fusion.3), kind=kOutput, calls=%fused_computation.clone.1 | convolution fusion | flops 1216217088 | bytes 7102468 | tf_op jit(solution)/shard_map/while/body/eval_jaxpr/dot_general | solution.py:54
  354.0 7.0 %select_add_fusion.4 = f32[768,1536]{1,0:T(8,128)} fusion(f32[768,1536]{1,0:T(8,128)} %multiply_reduce_fusion.4, f32[768,1536]{1,0:T(8,128)} %get-tuple-element.373, pred[]{:T(512)S(6)} %compare.13), kind=kLoop, calls=%fused_computation.1.clone.1 | loop fusion | flops 2359296 | bytes 14155777 | tf_op jit(solution)/shard_map/while/body/eval_jaxpr/add | solution.py:58
  362.9 6.6 %multiply_reduce_fusion.4 = f32[768,1536]{1,0:T(8,128)} fusion(f32[4,1536]{1,0:T(4,128)S(1)} %bitcast.204, bf16[32,128,1536]{2,1,0:T(8,128)(2,1)} %get-tuple-element.384, s32[]{:T(128)S(6)} %select_n.66, bf16[768,4,128]{2,1,0:T(4,128)(2,1)S(1)} %constant_dynamic-slice_fusion.3), kind=kOutput, calls=%fused_computation.clone.1 | convolution fusion | flops 1216217088 | bytes 7102468 | tf_op jit(solution)/shard_map/while/body/eval_jaxpr/dot_general | solution.py:54
  369.5 7.0 %select_add_fusion.4 = f32[768,1536]{1,0:T(8,128)} fusion(f32[768,1536]{1,0:T(8,128)} %multiply_reduce_fusion.4, f32[768,1536]{1,0:T(8,128)} %get-tuple-element.373, pred[]{:T(512)S(6)} %compare.13), kind=kLoop, calls=%fused_computation.1.clone.1 | loop fusion | flops 2359296 | bytes 14155777 | tf_op jit(solution)/shard_map/while/body/eval_jaxpr/add | solution.py:58
  376.5 6.1 %copy.128 = f32[768,1536]{0,1:T(8,128)} copy(f32[768,1536]{1,0:T(8,128)} %get-tuple-element.193) | data formatting | bytes 9437184 | tf_op jit(solution)/shard_map/while | solution.py:61
  385.7 73.0 %while.29 = (s32[]{:T(128)}, f32[768,4096]{1,0:T(8,128)}, bf16[768,6,128]{0,2,1:T(8,128)(2,1)S(1)}, bf16[4096,6,128]{0,2,1:T(8,128)(2,1)}, bf16[32,6]{0,1:T(8,12...) while((s32[]{:T(128)}, f32[768,4096]{1,0:T(8,128)}, ...), condition=%wide.region_10.11_spmd.clone, body=%wide.region_8.10_spmd.clone.sunk | while | flops 1626341504 | bytes 52954904 | solution.py:84
  385.8 11.2 %multiply_reduce_fusion.5 = f32[768,4096]{1,0:T(8,128)} fusion(f32[2,4096]{1,0:T(2,128)S(1)} %bitcast.203, bf16[4096,6,128]{0,2,1:T(8,128)(2,1)} %get-tuple-element.411, s32[]{:T(128)S(6)} %select_n.67, bf16[768,6,128]{0,2,1:T(8,128)(2,1)S(1)} %get-tuple-element.410), kind=kOutput, calls=%fused_computation.9.clone.1 | convolution fusion | flops 1620049920 | bytes 15107072 | tf_op jit(solution)/shard_map/while/body/eval_jaxpr/dot_general | solution.py:77
  397.0 10.9 %select_add_fusion.5 = f32[768,4096]{1,0:T(8,128)} fusion(f32[768,4096]{1,0:T(8,128)} %multiply_reduce_fusion.5, f32[768,4096]{1,0:T(8,128)} %get-tuple-element.400, pred[]{:T(512)S(6)} %compare.14), kind=kLoop, calls=%fused_computation.10.clone.1 | loop fusion | flops 6291456 | bytes 37748736 | tf_op jit(solution)/shard_map/while/body/eval_jaxpr/add | solution.py:81
  408.0 11.2 %multiply_reduce_fusion.5 = f32[768,4096]{1,0:T(8,128)} fusion(f32[2,4096]{1,0:T(2,128)S(1)} %bitcast.203, bf16[4096,6,128]{0,2,1:T(8,128)(2,1)} %get-tuple-element.411, s32[]{:T(128)S(6)} %select_n.67, bf16[768,6,128]{0,2,1:T(8,128)(2,1)S(1)} %get-tuple-element.410), kind=kOutput, calls=%fused_computation.9.clone.1 | convolution fusion | flops 1620049920 | bytes 15107072 | tf_op jit(solution)/shard_map/while/body/eval_jaxpr/dot_general | solution.py:77
  419.2 14.1 %select_add_fusion.5 = f32[768,4096]{1,0:T(8,128)} fusion(f32[768,4096]{1,0:T(8,128)} %multiply_reduce_fusion.5, f32[768,4096]{1,0:T(8,128)} %get-tuple-element.400, pred[]{:T(512)S(6)} %compare.14), kind=kLoop, calls=%fused_computation.10.clone.1 | loop fusion | flops 6291456 | bytes 37748736 | tf_op jit(solution)/shard_map/while/body/eval_jaxpr/add | solution.py:81
  433.4 11.2 %multiply_reduce_fusion.5 = f32[768,4096]{1,0:T(8,128)} fusion(f32[2,4096]{1,0:T(2,128)S(1)} %bitcast.203, bf16[4096,6,128]{0,2,1:T(8,128)(2,1)} %get-tuple-element.411, s32[]{:T(128)S(6)} %select_n.67, bf16[768,6,128]{0,2,1:T(8,128)(2,1)S(1)} %get-tuple-element.410), kind=kOutput, calls=%fused_computation.9.clone.1 | convolution fusion | flops 1620049920 | bytes 15107072 | tf_op jit(solution)/shard_map/while/body/eval_jaxpr/dot_general | solution.py:77
  444.6 14.1 %select_add_fusion.5 = f32[768,4096]{1,0:T(8,128)} fusion(f32[768,4096]{1,0:T(8,128)} %multiply_reduce_fusion.5, f32[768,4096]{1,0:T(8,128)} %get-tuple-element.400, pred[]{:T(512)S(6)} %compare.14), kind=kLoop, calls=%fused_computation.10.clone.1 | loop fusion | flops 6291456 | bytes 37748736 | tf_op jit(solution)/shard_map/while/body/eval_jaxpr/add | solution.py:81
  458.7 8.1 %convert_element_type.187 = bf16[768,4096]{1,0:T(8,128)(2,1)} convert(f32[768,4096]{1,0:T(8,128)} %get-tuple-element.194) | non-fusion elementwise | flops 3145728 | bytes 18874368 | tf_op jit(solution)/shard_map/convert_element_type | solution.py:143
  466.8 6.7 %all-to-all-start.1 = ((bf16[32,24,4096]{2,1,0:T(8,128)(2,1)}), bf16[32,24,4096]{2,1,0:T(8,128)(2,1)}, u32[]{:S(2)}, u32[]{:S(2)}) async-start(bf16[32,24,4096]{2,1,0:T(8,128)(2,1)} %bitcast.189), calls=%async_computation.1 | async-start | bytes 12582912 | tf_op jit(solution)/shard_map/all_to_all | solution.py:144
  475.2 97.6 %all-to-all-done.1 = bf16[32,24,4096]{2,1,0:T(8,128)(2,1)} async-done(((bf16[32,24,4096]{2,1,0:T(8,128)(2,1)}), bf16[32,24,4096]{2,1,0:T(8,128)(2,1)}, u32[]{:S(2)}, u32[]{:S(2)}) %all-to-all-start.1) | async-done | bytes 6291488 | tf_op jit(solution)/shard_map/all_to_all | solution.py:144
  572.8 5.4 convolution_convert_fusion.1
  (109 shorter events, 59.9 us)
Async XLA Ops:
  6.5 70.2 %copy-start = (bf16[192,4096]{1,0:T(8,128)(2,1)S(1)}, bf16[192,4096]{1,0:T(8,128)(2,1)}, u32[]{:S(2)}) copy-start(bf16[192,4096]{1,0:T(8,128)(2,1)} %param.15) | copy-start | bytes 4718596
  6.5 229.8 %all-gather.3.cloned.1.call-start = ((), (), s32[]{:S(2)}) async-start(), calls=%async_computation.2 | async-start | bytes 15728640 | tf_op jit(solution)/shard_map/all_gather | solution.py:127
  47.9 4.6 copy-start.5
  60.7 1.9 copy-start.2
  60.7 2.8 copy-start.3
  63.5 9.4 %copy-start.12 = (s32[192,8]{0,1:T(8,128)S(1)}, s32[192,8]{0,1:T(8,128)}, u32[]{:S(2)}) copy-start(s32[192,8]{0,1:T(8,128)} %param.16) | copy-start | bytes 18436
  74.6 0.6 copy-start.10
  81.3 9.3 %copy-start.9 = (bf16[1,1024,768]{2,1,0:T(8,128)(2,1)S(1)}, bf16[1,1024,768]{2,1,0:T(8,128)(2,1)}, u32[]{:S(2)}) copy-start(bf16[1,1024,768]{2,1,0:T(8,128)(2,1)} %param.24) | copy-start | bytes 4718596
  81.3 112.5 %all-to-all-start = ((bf16[32,24,4096]{2,1,0:T(8,128)(2,1)}), bf16[32,24,4096]{2,1,0:T(8,128)(2,1)}, u32[]{:S(2)}, u32[]{:S(2)}) async-start(bf16[32,24,4096]{2,1,0:T(8,128)(2,1)} %bitcast.186), calls=%async_computation | async-start | bytes 12582912 | tf_op jit(solution)/shard_map/all_to_all | solution.py:132
  90.5 295.1 %all-gather.5.cloned.1.call-start = ((), (), s32[]{:S(2)}) async-start(), calls=%async_computation.3 | async-start | bytes 7864320 | tf_op jit(solution)/shard_map/all_gather | solution.py:129
  109.2 2.8 copy-start.7
  109.2 3.8 copy-start.8
  113.0 4.5 copy-start.6
  117.3 1.9 copy-start.4
  466.8 6.7 %copy-start.13 = (bf16[192,8]{0,1:T(8,128)(2,1)S(1)}, bf16[192,8]{0,1:T(8,128)(2,1)}, u32[]{:S(2)}) copy-start(bf16[192,8]{0,1:T(8,128)(2,1)} %param.17) | copy-start | bytes 9220
  466.8 6.8 %copy-start.11 = (s32[192,8]{1,0:T(8,128)S(1)}, s32[192,8]{1,0:T(8,128)}, u32[]{:S(2)}) copy-start(s32[192,8]{1,0:T(8,128)} %copy-done.10) | copy-start | bytes 18436
  466.8 106.0 %all-to-all-start.1 = ((bf16[32,24,4096]{2,1,0:T(8,128)(2,1)}), bf16[32,24,4096]{2,1,0:T(8,128)(2,1)}, u32[]{:S(2)}, u32[]{:S(2)}) async-start(bf16[32,24,4096]{2,1,0:T(8,128)(2,1)} %bitcast.189), calls=%async_computation.1 | async-start | bytes 12582912 | tf_op jit(solution)/shard_map/all_to_all | solution.py:144
  572.8 5.5 copy-start.1
Sparse Core Ops, SparseCore 0:
  73.0 163.2 all-gather.2
  238.0 48.8 all-gather.4
where the time goes:
time: 594 us; the launch traced here: 585 us
  other arithmetic  144 us (24%)
  waiting for transfers between devices  133 us (22%)
  local copies, waits for them, and re-layouts  110 us (19%)
  matrix products  97.8 us (16%)
  blocking collectives  70.7 us (12%)
  starting transfers between devices  16 us (3%)
  between operations  13.9 us (2%)
    all_to_all x1, waiting for transfers between devices, shards(): lax.all_to_all(output.reshape(arrived.shape), 'expert', split_axis=0, con...  97.6 us
    add x11, other arithmetic, add_blocks(): return total + jnp.sum(pieces * factor[:, None, :], axis=0)  93.7 us
    unnamed x48, local copies, waits for them, and re-layouts  86.8 us
    all_gather x1, blocking collectives, shards(): lax.all_gather(scale_lower, 'zero', axis=0, tiled=True)  64 us
    dot_general x8, matrix products, add_blocks(): lax.dot_general(rows, weights, (((2,), (1,)), ((1,), (0,))), preferred_el...  53.1 us
    all_gather x1, waiting for transfers between devices, shards(): lax.all_gather(quant_gate, 'zero', axis=0, tiled=True)  35.2 us
    dot_general x3, matrix products, add_blocks(): lax.dot_general(rows, weights, (((2,), (2,)), ((1,), (1,))), preferred_el...  33.6 us
    dynamic_slice x8, local copies, waits for them, and re-layouts, add_blocks(): rows = lax.dynamic_slice_in_dim(folded, first, width, 1)  14.5 us
  transfers between devices with their start and end apart: 4, of which 2 were waited for; matrix products, arithmetic and copies ran while one was open for 33% of the time, Pallas kernels for 0%

commit v1 on v0

v1 whole, which is shorter than its diff:
```python
import jax
import jax.numpy as jnp
from jax import lax
from jax.experimental import pallas as pl
from jax.experimental.pallas import tpu as pltpu
from jax.sharding import PartitionSpec as P

MESH = pl.DeviceIdType.MESH
F32 = jnp.float32
BF16 = jnp.bfloat16

TOK = 192
D = 4096
CAP = 24
PAIR = 2 * CAP
PLANE = 16
ROWS = PLANE * PAIR
GU = 1536
HW = 768
SHARD = 1024
CHUNKS = 4
DC = D // CHUNKS
PARTS = 4
PART = SHARD // PARTS

beta_one = 0.9
beta_two = 0.999
learn_rate = 0.002
adam_eps = 1e-08
corr_two = 0.63230457523

OFFSETS = (
    (2, 2), (1, 2), (3, 2), (2, 1), (2, 3), (1, 1), (3, 3), (1, 3), (3, 1),
    (2, 0), (0, 2), (1, 0), (3, 0), (0, 1), (0, 3),
)
PEERS = len(OFFSETS)


def remote(src, dst, send_sem, recv_sem, device):
    return pltpu.make_async_remote_copy(
        src_ref=src,
        dst_ref=dst,
        send_sem=send_sem,
        recv_sem=recv_sem,
        device_id=device,
        device_id_type=MESH,
    )


def chunk_of(zero, k):
    sibling = zero + 1 - 2 * (zero % 2)
    base = sibling if k % 2 else zero
    return (base + 2) % 4 if k >= 2 else base


def adam(master, grad, first, second):
    grads = grad.astype(F32)
    m_one = beta_one * first.astype(F32) + (1.0 - beta_one) * grads
    m_two = beta_two * second.astype(F32) + (1.0 - beta_two) * grads * grads
    return master - learn_rate * m_one / (jnp.sqrt(m_two * (1.0 / corr_two)) + adam_eps)


def cast_block(block):
    largest = jnp.max(jnp.max(jnp.abs(block), axis=0, keepdims=True), axis=1, keepdims=True)
    scale = ((largest + 1e-06) / 448.0).astype(BF16).astype(F32)
    return (block * (1.0 / scale)).astype(BF16), scale


def kernel(
    tokens, ids, weights,
    mgu, ggu, fgu, vgu, mdn, gdn, fdn, vdn,
    out,
    tokv, pk, pks, sel, comb, og, xr, wgu, wdn, scg, scd, acc, hid, ret, ps, pr,
    am, ag, af, av, bm, bg, bf, bv,
    tok_l, tok_s, tok_r, pk_s, pk_r, dis_l, dis_s, dis_r, ret_l, ret_s, ret_r,
    wg_s, wg_r, wd_s, wd_r, sc_s, sc_r, par_s, par_r, a_sem, b_sem, out_sem,
):
    expert = lax.axis_index("expert")
    zero = lax.axis_index("zero")
    x, zz, yl = expert // 8, (expert // 2) % 4, expert % 2
    yh, core = zero // 2, zero % 2
    y = yh * 2 + yl
    pe = x * 4 + zz
    step = 1 - 2 * core

    def at(px, py, pz, pc):
        return (px * 8 + pz * 2 + py % 2, (py // 2) * 2 + pc)

    y_to, y_from = (y + step + 4) % 4, (y - step + 4) % 4
    to_dev = at(x, y_to, zz, core)
    from_dev = at(x, y_from, zz, core)
    sib_dev = at(x, y, zz, 1 - core)
    far_dev = at(x, (y + 2) % 4, zz, core)
    zero_to = (y_to // 2) * 2 + core

    peers = []
    sources = []
    for dx, dz in OFFSETS:
        px, pz = (x + dx) % 4, (zz + dz) % 4
        qx, qz = (x + 4 - dx) % 4, (zz + 4 - dz) % 4
        peers.append((at(px, y, pz, core), px * 4 + pz))
        sources.append(qx * 4 + qz)

    def slot_rows(p):
        return pl.ds(pl.multiple_of(p * PAIR, 16), PAIR)

    def columns(zero_index, k):
        return pl.ds(pl.multiple_of(chunk_of(zero_index, k) * DC, DC), DC)

    own_tok = []
    for k in range(CHUNKS):
        copy = pltpu.make_async_copy(
            tokens.at[:, columns(zero, k)], tokv.at[k, pl.ds(0, TOK)], tok_l.at[k]
        )
        copy.start()
        own_tok.append(copy)

    def gu_loads(chunk):
        slot = chunk % 2
        rows = pl.ds(pl.multiple_of(chunk * 128, 128), 128)
        return [
            pltpu.make_async_copy(src.at[0, rows], dst.at[slot], a_sem.at[slot, i])
            for i, (src, dst) in enumerate(((mgu, am), (ggu, ag), (fgu, af), (vgu, av)))
        ]

    def dn_loads(chunk):
        slot = chunk % 2
        rows = pl.ds(pl.multiple_of(chunk * 128, 128), 128)
        return [
            pltpu.make_async_copy(src.at[0, rows], dst.at[slot], b_sem.at[slot, i])
            for i, (src, dst) in enumerate(((mdn, bm), (gdn, bg), (fdn, bf), (vdn, bv)))
        ]

    for chunk in range(2):
        for copy in gu_loads(chunk):
            copy.start()
    for chunk in range(2):
        for copy in dn_loads(chunk):
            copy.start()

    lane = lax.broadcasted_iota(jnp.int32, (TOK, 128), 1)
    mine = jnp.zeros((TOK, 128), F32)
    theirs = jnp.zeros((TOK, 128), F32)
    for k in range(8):
        named = ids[:, k : k + 1]
        weight = weights[:, k : k + 1].astype(F32)
        for other in range(2):
            row = yl if other == 0 else 1 - yl
            value = jnp.where(
                named == lane * 8 + 4 * row,
                weight,
                jnp.where(named == (lane - 64) * 8 + 4 * row, 1.0, 0.0),
            )
            if other == 0:
                mine = mine + value
            else:
                theirs = theirs + value
    pk[0:TOK, :] = mine
    pks[...] = theirs

    barrier = pltpu.get_barrier_semaphore()
    greeted = [dev for dev, _ in peers] + [sib_dev, far_dev, to_dev, from_dev]
    for dev in greeted:
        pl.semaphore_signal(barrier, inc=1, device_id=dev, device_id_type=MESH)
    pl.semaphore_wait(barrier, len(greeted))

    sends = []

    def start(copy):
        copy.start()
        sends.append(copy)
        return copy

    pk_copy = start(remote(pks, pk.at[pl.ds(TOK, TOK)], pk_s, pk_r, to_dev))
    tok_copy = [
        start(
            remote(
                tokens.at[:, columns(zero_to, k)],
                tokv.at[k, pl.ds(TOK, TOK)],
                tok_s.at[k],
                tok_r.at[k],
                to_dev,
            )
        )
        for k in range(CHUNKS)
    ]

    eighth = lax.broadcasted_iota(jnp.int32, (8, 128), 0)
    scg[0] = jnp.zeros((8, GU), F32)
    scd[0] = jnp.zeros((8, SHARD), F32)

    def adam_gu(chunk, carry):
        slot = chunk % 2
        for copy in gu_loads(chunk):
            copy.wait()
        rows = pl.ds(pl.multiple_of(chunk * 128, 128), 128)

        def column_pair(n, inner):
            cols = pl.ds(pl.multiple_of(n * 256, 256), 256)
            fresh = adam(am[slot, :, cols], ag[slot, :, cols], af[slot, :, cols], av[slot, :, cols])
            for h in range(2):
                quant, scale = cast_block(fresh[:, h * 128 : h * 128 + 128])
                half = pl.ds(pl.multiple_of(n * 256 + h * 128, 128), 128)
                wgu[0, rows, half] = quant
                scg[0, :, half] = jnp.where(eighth == chunk, scale, scg[0, :, half])
            return inner

        lax.fori_loop(0, GU // 256, column_pair, 0)

        @pl.when(chunk + 2 < SHARD // 128)
        def _():
            for copy in gu_loads(chunk + 2):
                copy.start()

        return carry

    def adam_dn(chunk, carry):
        slot = chunk % 2
        for copy in dn_loads(chunk):
            copy.wait()
        rows = pl.ds(pl.multiple_of(chunk * 128, 128), 128)
        for n in range(HW // 256):
            cols = slice(n * 256, n * 256 + 256)
            fresh = adam(bm[slot, :, cols], bg[slot, :, cols], bf[slot, :, cols], bv[slot, :, cols])
            for h in range(2):
                block = 2 * n + h
                quant, scale = cast_block(fresh[:, h * 128 : h * 128 + 128])
                wdn[0, rows, block * 128 : block * 128 + 128] = quant
                scd[0, block : block + 1, rows] = jnp.broadcast_to(scale, (1, 128))

        @pl.when(chunk + 2 < SHARD // 128)
        def _():
            for copy in dn_loads(chunk + 2):
                copy.start()

        return carry

    def part_rows(p):
        return pl.ds(p * PART, PART)

    gu_sib, gu_far = [], []

    def send_gu(p):
        rows = part_rows(p)
        gu_far.append(
            start(remote(wgu.at[0, rows], wgu.at[2, rows], wg_s.at[1, p], wg_r.at[1, p], far_dev))
        )
        gu_sib.append(
            start(remote(wgu.at[0, rows], wgu.at[1, rows], wg_s.at[0, p], wg_r.at[0, p], sib_dev))
        )

    def build_maps():
        pk_copy.wait_recv()
        packed = pk[...]
        place = lax.broadcasted_iota(jnp.int32, (128, ROWS), 0)
        slot_no = lax.broadcasted_iota(jnp.int32, (128, ROWS), 1)
        lowest = (place - 64) * PAIR
        spread_slot = jnp.where((slot_no >= lowest) & (slot_no < lowest + PAIR), 1.0, 0.0).astype(BF16)
        low_weight = place * PAIR
        spread_weight = jnp.where(
            (slot_no >= low_weight) & (slot_no < low_weight + PAIR), 1.0, 0.0
        ).astype(BF16)
        t_row = lax.broadcasted_iota(jnp.int32, (2 * TOK, 2 * TOK), 0)
        t_col = lax.broadcasted_iota(jnp.int32, (2 * TOK, 2 * TOK), 1)
        same = (t_row >= TOK) == (t_col >= TOK)
        earlier = jnp.where((t_col < t_row) & same, 1.0, 0.0).astype(BF16)
        flags = packed.astype(BF16)
        counted = jnp.dot(earlier, flags, preferred_element_type=F32)
        token = lax.broadcasted_iota(jnp.int32, (2 * TOK, 128), 0)
        slot = counted + jnp.where(token >= TOK, float(CAP), 0.0)
        lanes = lax.broadcasted_iota(jnp.int32, (2 * TOK, 128), 1)
        chosen = (packed > 0.5) & (lanes >= 64)
        slot = jnp.where(chosen, slot, jnp.where(lanes >= 64, -1.0, 0.0)).astype(BF16)
        route = jnp.where(lanes < 64, packed, 0.0).astype(BF16)

        wide = lax.broadcasted_iota(jnp.int32, (1, ROWS), 1)
        within = wide
        for p in range(1, PLANE):
            within = within - jnp.where(wide >= p * PAIR, PAIR, 0)
        slots_wide = jnp.dot(slot, spread_slot, preferred_element_type=F32)
        route_wide = jnp.dot(route, spread_weight, preferred_element_type=F32)
        hit = slots_wide == within.astype(F32)
        comb[...] = jnp.where(hit, route_wide, 0.0).astype(BF16)
        sel[...] = jnp.transpose(jnp.where(hit, 1.0, 0.0)).astype(BF16)

    dispatched = [[] for _ in range(CHUNKS)]
    kept = []

    def dispatch(k):
        own_tok[k].wait()
        tok_copy[k].wait_recv()

        def column_tile(n, carry):
            cols = pl.ds(pl.multiple_of(n * 256, 256), 256)
            og[k, :, cols] = jnp.dot(
                sel[...], tokv[k, :, cols], preferred_element_type=F32
            ).astype(BF16)
            return carry

        lax.fori_loop(0, DC // 256, column_tile, 0)
        for i, (dev, p) in enumerate(peers):
            copy = remote(
                og.at[k, slot_rows(p)], xr.at[k, slot_rows(pe)], dis_s.at[k, i], dis_r.at[k, i], dev
            )
            copy.start()
            dispatched[k].append(copy)
        copy = pltpu.make_async_copy(og.at[k, slot_rows(pe)], xr.at[k, slot_rows(pe)], dis_l.at[k])
        copy.start()
        kept.append(copy)

    def arrived(k):
        kept[k].wait()
        for i, p in enumerate(sources):
            remote(
                og.at[k, slot_rows(p)],
                xr.at[k, slot_rows(p)],
                dis_s.at[k, i],
                dis_r.at[k, i],
                peers[i][0],
            ).wait_recv()

    lax.fori_loop(0, 2, adam_gu, 0)
    send_gu(0)
    build_maps()
    dispatch(0)
    lax.fori_loop(2, 4, adam_gu, 0)
    send_gu(1)
    dispatch(1)
    lax.fori_loop(4, 6, adam_gu, 0)
    send_gu(2)
    dispatch(2)
    lax.fori_loop(6, 8, adam_gu, 0)
    scg_far = start(remote(scg.at[0], scg.at[2], sc_s.at[1], sc_r.at[1], far_dev))
    scg_sib = start(remote(scg.at[0], scg.at[1], sc_s.at[0], sc_r.at[0], sib_dev))
    send_gu(3)
    dispatch(3)
    lax.fori_loop(0, 8, adam_dn, 0)
    scd_far = start(remote(scd.at[0], scd.at[2], sc_s.at[4], sc_r.at[4], far_dev))
    scd_sib = start(remote(scd.at[0], scd.at[1], sc_s.at[3], sc_r.at[3], sib_dev))
    dn_sib = start(remote(wdn.at[0], wdn.at[1], wd_s.at[0, 0], wd_r.at[0, 0], sib_dev))

    gu_fwd, dn_far, dn_fwd = [], [], []

    def forward_gu(p):
        gu_far[p].wait_recv()
        rows = part_rows(p)
        gu_fwd.append(
            start(remote(wgu.at[2, rows], wgu.at[3, rows], wg_s.at[2, p], wg_r.at[2, p], sib_dev))
        )

    def dn_rows(p):
        return pl.ds(p * 512, 512)

    def send_dn(p):
        rows = dn_rows(p)
        dn_far.append(
            start(remote(wdn.at[0, rows], wdn.at[2, rows], wd_s.at[1, p], wd_r.at[1, p], far_dev))
        )

    def forward_dn(p):
        dn_far[p].wait_recv()
        rows = dn_rows(p)
        dn_fwd.append(
            start(remote(wdn.at[2, rows], wdn.at[3, rows], wd_s.at[2, p], wd_r.at[2, p], sib_dev))
        )

    def gated(k, blocks, begin=False):
        def column_tile(n, carry):
            cols = pl.ds(pl.multiple_of(n * 256, 256), 256)
            total = None if begin else acc[:, cols]
            for b in blocks:
                inner = slice(b * 128, b * 128 + 128)
                piece = jnp.dot(
                    xr[k, :, inner], wgu[k, inner, cols], preferred_element_type=F32
                ) * scg[k, b : b + 1, cols]
                total = piece if total is None else total + piece
            acc[:, cols] = total
            return carry

        lax.fori_loop(0, GU // 256, column_tile, 0)

    arrived(0)
    gated(0, range(8), begin=True)
    forward_gu(0)
    scg_far.wait_recv()
    scg_fwd = start(remote(scg.at[2], scg.at[3], sc_s.at[2], sc_r.at[2], sib_dev))
    scg_sib.wait_recv()
    for p in range(PARTS):
        gu_sib[p].wait_recv()
    arrived(1)
    gated(1, range(8))
    forward_gu(1)
    arrived(2)
    gated(2, range(4))
    forward_gu(2)
    send_dn(0)
    gated(2, range(4, 6))
    arrived(3)
    scg_fwd.wait_recv()
    for p in range(3):
        gu_fwd[p].wait_recv()
    gated(3, range(6))
    forward_gu(3)
    send_dn(1)
    gated(2, range(6, 8))
    gu_fwd[3].wait_recv()
    gated(3, range(6, 8))

    def activate(n, carry):
        cols = pl.ds(pl.multiple_of(n * 256, 256), 256)
        gate = acc[:, cols]
        up = acc[:, pl.ds(pl.multiple_of(HW + n * 256, 256), 256)]
        hid[:, cols] = (gate / (1.0 + jnp.exp(-gate)) * up).astype(BF16)
        return carry

    lax.fori_loop(0, HW // 256, activate, 0)

    returned = []

    def lower(k):
        for copy in dispatched[k]:
            copy.wait_send()

        def row_tile(n, carry):
            cols = pl.ds(pl.multiple_of(n * 256, 256), 256)
            total = None
            for c in range(HW // 128):
                inner = slice(c * 128, c * 128 + 128)
                piece = lax.dot_general(
                    hid[:, inner],
                    wdn[k, cols, inner],
                    (((1,), (1,)), ((), ())),
                    preferred_element_type=F32,
                ) * scd[k, c : c + 1, cols]
                total = piece if total is None else total + piece
            og[k, :, cols] = total.astype(BF16)
            return carry

        lax.fori_loop(0, DC // 256, row_tile, 0)
        for i, (dev, p) in enumerate(peers):
            start(
                remote(
                    og.at[k, slot_rows(p)],
                    ret.at[k, slot_rows(pe)],
                    ret_s.at[k, i],
                    ret_r.at[k, i],
                    dev,
                )
            )
        copy = pltpu.make_async_copy(og.at[k, slot_rows(pe)], ret.at[k, slot_rows(pe)], ret_l.at[k])
        copy.start()
        returned.append(copy)

    partial = []

    def mix(k):
        returned[k].wait()
        for i, p in enumerate(sources):
            remote(
                og.at[k, slot_rows(p)],
                ret.at[k, slot_rows(p)],
                ret_s.at[k, i],
                ret_r.at[k, i],
                peers[i][0],
            ).wait_recv()

        def column_tile(n, carry):
            cols = pl.ds(pl.multiple_of(n * 256, 256), 256)
            both = jnp.dot(comb[...], ret[k, :, cols], preferred_element_type=F32)
            acc[k * TOK : (k + 1) * TOK, cols] = both[:TOK]
            ps[k, :, cols] = both[TOK:].astype(BF16)
            return carry

        lax.fori_loop(0, DC // 256, column_tile, 0)
        partial.append(start(remote(ps.at[k], pr.at[k], par_s.at[k], par_r.at[k], from_dev)))

    written = []
    apart = (y_to // 2 - yh) * (y_to // 2 - yh)

    def finish(k):
        partial[k].wait_recv()
        here = k + 2 * apart * (1 - 2 * (k // 2))
        rows = pl.ds(pl.multiple_of(here * TOK, TOK), TOK)
        tokv[k, 0:TOK, :] = (acc[rows, 0:DC] + pr[k].astype(F32)).astype(BF16)
        copy = pltpu.make_async_copy(
            tokv.at[k, pl.ds(0, TOK)], out.at[:, columns(zero_to, k)], out_sem.at[k]
        )
        copy.start()
        written.append(copy)

    lower(0)
    scd_sib.wait_recv()
    dn_sib.wait_recv()
    lower(1)
    scd_far.wait_recv()
    scd_fwd = start(remote(scd.at[2], scd.at[3], sc_s.at[5], sc_r.at[5], sib_dev))
    forward_dn(0)
    forward_dn(1)
    lower(2)
    scd_fwd.wait_recv()
    for p in range(2):
        dn_fwd[p].wait_recv()
    lower(3)
    mix(0)
    mix(1)
    mix(2)
    finish(0)
    mix(3)
    finish(2)
    finish(1)
    finish(3)
    for copy in sends:
        copy.wait_send()
    for copy in written:
        copy.wait()


def shards(*args):
    any_spec = pl.BlockSpec(memory_space=pl.ANY)
    vmem_spec = pl.BlockSpec(memory_space=pltpu.VMEM)
    dma = pltpu.SemaphoreType.DMA
    scratch = [
        pltpu.VMEM((CHUNKS, 2 * TOK, DC), BF16),
        pltpu.VMEM((2 * TOK, 128), F32),
        pltpu.VMEM((TOK, 128), F32),
        pltpu.VMEM((ROWS, 2 * TOK), BF16),
        pltpu.VMEM((2 * TOK, ROWS), BF16),
        pltpu.VMEM((CHUNKS, ROWS, DC), BF16),
        pltpu.VMEM((CHUNKS, ROWS, DC), BF16),
        pltpu.VMEM((4, SHARD, GU), BF16),
        pltpu.VMEM((4, SHARD, HW), BF16),
        pltpu.VMEM((4, 8, GU), F32),
        pltpu.VMEM((4, 8, SHARD), F32),
        pltpu.VMEM((ROWS, GU), F32),
        pltpu.VMEM((ROWS, HW), BF16),
        pltpu.VMEM((CHUNKS, ROWS, DC), BF16),
        pltpu.VMEM((CHUNKS, TOK, DC), BF16),
        pltpu.VMEM((CHUNKS, TOK, DC), BF16),
        pltpu.VMEM((2, 128, GU), F32),
        pltpu.VMEM((2, 128, GU), BF16),
        pltpu.VMEM((2, 128, GU), BF16),
        pltpu.VMEM((2, 128, GU), BF16),
        pltpu.VMEM((2, 128, HW), F32),
        pltpu.VMEM((2, 128, HW), BF16),
        pltpu.VMEM((2, 128, HW), BF16),
        pltpu.VMEM((2, 128, HW), BF16),
        dma((CHUNKS,)), dma((CHUNKS,)), dma((CHUNKS,)),
        dma, dma,
        dma((CHUNKS,)), dma((CHUNKS, PEERS)), dma((CHUNKS, PEERS)),
        dma((CHUNKS,)), dma((CHUNKS, PEERS)), dma((CHUNKS, PEERS)),
        dma((3, PARTS)), dma((3, PARTS)), dma((3, 2)), dma((3, 2)),
        dma((6,)), dma((6,)),
        dma((CHUNKS,)), dma((CHUNKS,)),
        dma((2, 4)), dma((2, 4)), dma((CHUNKS,)),
    ]
    return pl.pallas_call(
        kernel,
        name="layer",
        out_shape=jax.ShapeDtypeStruct((TOK, D), BF16),
        in_specs=[any_spec, vmem_spec, vmem_spec] + [any_spec] * 8,
        out_specs=any_spec,
        scratch_shapes=scratch,
        compiler_params=pltpu.CompilerParams(
            collective_id=0, has_side_effects=True, vmem_limit_bytes=60 * 1024 * 1024
        ),
        cost_estimate=pl.CostEstimate(
            flops=17_000_000_000, bytes_accessed=30_000_000, transcendentals=5_000_000
        ),
    )(*args)


def solution(mesh):
    rows = P(("expert", "zero"), None)
    weight = P("expert", "zero", None)
    in_specs = (rows,) * 3 + (weight,) * 8
    return jax.shard_map(shards, mesh=mesh, in_specs=in_specs, out_specs=rows, check_vma=False)
```

time: 594 us -> 260 us (0.44)
  the two profiles are of different devices: /device:TPU:32 before, /device:TPU:8 now
where the time goes in v1:
time: 260 us; the launch traced here: 256 us
  Pallas kernels  250 us (96%)
  local copies, waits for them, and re-layouts  5.58 us (2%)
    pallas_call x1, Pallas kernels, shards(): pl.pallas_call(kernel, name='layer', out_shape=jax.ShapeDtypeStruct((TOK,...  250 us
    unnamed x3, local copies, waits for them, and re-layouts  5.58 us

profile of v1, /device:TPU:8, one launch (start us, length us, event | category | flops | bytes accessed | tf_op | source)
XLA Modules:
  0.0 255.7 jit_solution(10397926226071776769)
XLA Ops:
  0.0 1.4 copy.13.weights
  1.4 1.5 copy.12.ids
  2.9 250.1 %layer.1 = bf16[192,4096]{1,0:T(8,128)(2,1)} custom-call(bf16[192,4096]{1,0:T(8,128)(2,1)} %tokens.1, s32[192,8]{1,0:T(8,128)} %copy.12.ids, bf16[192,8]{1,0:T(8,128)(2,1)} %copy.13.weights, f32[1,1024,1536]{2,1,0:T(8,128)} %mgu.1, bf16[1,1024,1536]{2,1,0:T(8,128)(2,1)} %ggu.1, bf16[1,1024,1536]{2,1,0:T(8,128)(2,1)} %fgu.1, bf16[1,1024,1536]{2,1,0:T(8,128)(2,1)} %vgu.1, ...), custom_call_target="tpu_custom_call" | custom-call | flops 16999999488 | bytes 30000000 | tf_op jit(solution)/shard_map/layer/pallas_call | solution.py:556
  253.0 2.7 %copy.15 = bf16[192,4096]{1,0:T(8,128)(2,1)} copy(bf16[192,4096]{1,0:T(8,128)(2,1)} %layer.1) | data formatting | bytes 3145728

commit v2 on v1

--- a/solution.py
+++ b/solution.py
@@ -55,15 +55,36 @@
 
 def adam(master, grad, first, second):
     grads = grad.astype(F32)
-    m_one = beta_one * first.astype(F32) + (1.0 - beta_one) * grads
-    m_two = beta_two * second.astype(F32) + (1.0 - beta_two) * grads * grads
-    return master - learn_rate * m_one / (jnp.sqrt(m_two * (1.0 / corr_two)) + adam_eps)
-
-
-def cast_block(block):
-    largest = jnp.max(jnp.max(jnp.abs(block), axis=0, keepdims=True), axis=1, keepdims=True)
-    scale = ((largest + 1e-06) / 448.0).astype(BF16).astype(F32)
-    return (block * (1.0 / scale)).astype(BF16), scale
+    move = (learn_rate * beta_one) * first.astype(F32) + (learn_rate * (1.0 - beta_one)) * grads
+    spread = (beta_two / corr_two) * second.astype(F32) + ((1.0 - beta_two) / corr_two) * grads * grads
+    below = spread * lax.rsqrt(spread) + adam_eps
+    inverse = pl.reciprocal(below, approx=True)
+    inverse = inverse * (2.0 - below * inverse)
+    return master - move * inverse
+
+
+def fresh_chunk(master, grad, first, second, inv, slot, width, quant, put_scale):
+    def update(r, best):
+        rows = pl.ds(pl.multiple_of(r * 16, 16), 16)
+        fresh = adam(master[slot, rows, :], grad[slot, rows, :], first[slot, rows, :], second[slot, rows, :])
+        master[slot, rows, :] = fresh
+        size = jnp.abs(fresh)
+        return jnp.maximum(best, jnp.maximum(size[:8], size[8:]))
+
+    best = lax.fori_loop(0, 8, update, jnp.zeros((8, width), F32))
+    for b in range(width // 128):
+        cols = slice(b * 128, b * 128 + 128)
+        largest = jnp.max(jnp.max(best[:, cols], axis=0, keepdims=True), axis=1, keepdims=True)
+        scale = ((largest + 1e-06) / 448.0).astype(BF16).astype(F32)
+        put_scale(b, scale)
+        inv[:, cols] = jnp.broadcast_to(1.0 / scale, (8, 128))
+
+    def cast(r, carry):
+        rows = pl.ds(pl.multiple_of(r * 16, 16), 16)
+        quant(rows, (master[slot, rows, :] * inv[0:1, 0:width]).astype(BF16), r)
+        return carry
+
+    lax.fori_loop(0, 8, cast, 0)
 
 
 def kernel(
@@ -71,7 +92,7 @@
     mgu, ggu, fgu, vgu, mdn, gdn, fdn, vdn,
     out,
     tokv, pk, pks, sel, comb, og, xr, wgu, wdn, scg, scd, acc, hid, ret, ps, pr,
-    am, ag, af, av, bm, bg, bf, bv,
+    am, ag, af, av, bm, bg, bf, bv, inv,
     tok_l, tok_s, tok_r, pk_s, pk_r, dis_l, dis_s, dis_r, ret_l, ret_s, ret_r,
     wg_s, wg_r, wd_s, wd_r, sc_s, sc_r, par_s, par_r, a_sem, b_sem, out_sem,
 ):
@@ -171,41 +192,39 @@
         sends.append(copy)
         return copy
 
+    apart = (y_to // 2 - yh) * (y_to // 2 - yh)
+    for k in range(CHUNKS):
+        own_tok[k].wait()
     pk_copy = start(remote(pks, pk.at[pl.ds(TOK, TOK)], pk_s, pk_r, to_dev))
     tok_copy = [
-        start(
-            remote(
-                tokens.at[:, columns(zero_to, k)],
+        remote(
+                tokv.at[k + 2 * apart * (1 - 2 * (k // 2)), pl.ds(0, TOK)],
                 tokv.at[k, pl.ds(TOK, TOK)],
                 tok_s.at[k],
                 tok_r.at[k],
                 to_dev,
-            )
         )
         for k in range(CHUNKS)
     ]
+    for copy in tok_copy:
+        copy.start()
 
     eighth = lax.broadcasted_iota(jnp.int32, (8, 128), 0)
     scg[0] = jnp.zeros((8, GU), F32)
     scd[0] = jnp.zeros((8, SHARD), F32)
 
     def adam_gu(chunk, carry):
-        slot = chunk % 2
         for copy in gu_loads(chunk):
             copy.wait()
-        rows = pl.ds(pl.multiple_of(chunk * 128, 128), 128)
-
-        def column_pair(n, inner):
-            cols = pl.ds(pl.multiple_of(n * 256, 256), 256)
-            fresh = adam(am[slot, :, cols], ag[slot, :, cols], af[slot, :, cols], av[slot, :, cols])
-            for h in range(2):
-                quant, scale = cast_block(fresh[:, h * 128 : h * 128 + 128])
-                half = pl.ds(pl.multiple_of(n * 256 + h * 128, 128), 128)
-                wgu[0, rows, half] = quant
-                scg[0, :, half] = jnp.where(eighth == chunk, scale, scg[0, :, half])
-            return inner
-
-        lax.fori_loop(0, GU // 256, column_pair, 0)
+
+        def quant(rows, value, r):
+            wgu[0, pl.ds(pl.multiple_of(chunk * 128 + r * 16, 16), 16), :] = value
+
+        def put_scale(b, scale):
+            cols = slice(b * 128, b * 128 + 128)
+            scg[0, :, cols] = jnp.where(eighth == chunk, scale, scg[0, :, cols])
+
+        fresh_chunk(am, ag, af, av, inv, chunk % 2, GU, quant, put_scale)
 
         @pl.when(chunk + 2 < SHARD // 128)
         def _():
@@ -215,18 +234,17 @@
         return carry
 
     def adam_dn(chunk, carry):
-        slot = chunk % 2
         for copy in dn_loads(chunk):
             copy.wait()
-        rows = pl.ds(pl.multiple_of(chunk * 128, 128), 128)
-        for n in range(HW // 256):
-            cols = slice(n * 256, n * 256 + 256)
-            fresh = adam(bm[slot, :, cols], bg[slot, :, cols], bf[slot, :, cols], bv[slot, :, cols])
-            for h in range(2):
-                block = 2 * n + h
-                quant, scale = cast_block(fresh[:, h * 128 : h * 128 + 128])
-                wdn[0, rows, block * 128 : block * 128 + 128] = quant
-                scd[0, block : block + 1, rows] = jnp.broadcast_to(scale, (1, 128))
+        cols = pl.ds(pl.multiple_of(chunk * 128, 128), 128)
+
+        def quant(rows, value, r):
+            wdn[0, pl.ds(pl.multiple_of(chunk * 128 + r * 16, 16), 16), :] = value
+
+        def put_scale(b, scale):
+            scd[0, b : b + 1, cols] = jnp.broadcast_to(scale, (1, 128))
+
+        fresh_chunk(bm, bg, bf, bv, inv, chunk % 2, HW, quant, put_scale)
 
         @pl.when(chunk + 2 < SHARD // 128)
         def _():
@@ -287,7 +305,6 @@
     kept = []
 
     def dispatch(k):
-        own_tok[k].wait()
         tok_copy[k].wait_recv()
 
         def column_tile(n, carry):
@@ -320,20 +337,20 @@
             ).wait_recv()
 
     lax.fori_loop(0, 2, adam_gu, 0)
-    send_gu(0)
     build_maps()
     dispatch(0)
     lax.fori_loop(2, 4, adam_gu, 0)
-    send_gu(1)
     dispatch(1)
     lax.fori_loop(4, 6, adam_gu, 0)
-    send_gu(2)
     dispatch(2)
     lax.fori_loop(6, 8, adam_gu, 0)
+    dispatch(3)
     scg_far = start(remote(scg.at[0], scg.at[2], sc_s.at[1], sc_r.at[1], far_dev))
     scg_sib = start(remote(scg.at[0], scg.at[1], sc_s.at[0], sc_r.at[0], sib_dev))
+    send_gu(0)
+    send_gu(1)
+    send_gu(2)
     send_gu(3)
-    dispatch(3)
     lax.fori_loop(0, 8, adam_dn, 0)
     scd_far = start(remote(scd.at[0], scd.at[2], sc_s.at[4], sc_r.at[4], far_dev))
     scd_sib = start(remote(scd.at[0], scd.at[1], sc_s.at[3], sc_r.at[3], sib_dev))
@@ -475,7 +492,6 @@
         partial.append(start(remote(ps.at[k], pr.at[k], par_s.at[k], par_r.at[k], from_dev)))
 
     written = []
-    apart = (y_to // 2 - yh) * (y_to // 2 - yh)
 
     def finish(k):
         partial[k].wait_recv()
@@ -488,6 +504,8 @@
         copy.start()
         written.append(copy)
 
+    for copy in tok_copy:
+        copy.wait_send()
     lower(0)
     scd_sib.wait_recv()
     dn_sib.wait_recv()
@@ -544,6 +562,7 @@
         pltpu.VMEM((2, 128, HW), BF16),
         pltpu.VMEM((2, 128, HW), BF16),
         pltpu.VMEM((2, 128, HW), BF16),
+        pltpu.VMEM((8, GU), F32),
         dma((CHUNKS,)), dma((CHUNKS,)), dma((CHUNKS,)),
         dma, dma,
         dma((CHUNKS,)), dma((CHUNKS, PEERS)), dma((CHUNKS, PEERS)),

time: 260 us -> 210 us (0.81); the launches traced: 256 us -> 209 us
  Pallas kernels: 250 us -> 204 us
    pallas_call x1, Pallas kernels: 250 us -> 204 us  [shards(): pl.pallas_call(kernel, name='layer', out_shape=jax.ShapeDtypeStruct((TOK,...]
where the time goes in v2:
time: 210 us; the launch traced here: 209 us
  Pallas kernels  204 us (97%)
  local copies, waits for them, and re-layouts  5.58 us (3%)
    pallas_call x1, Pallas kernels, shards(): pl.pallas_call(kernel, name='layer', out_shape=jax.ShapeDtypeStruct((TOK,...  204 us
    unnamed x3, local copies, waits for them, and re-layouts  5.58 us

profile of v2, /device:TPU:8, one launch (start us, length us, event | category | flops | bytes accessed | tf_op | source)
XLA Modules:
  0.0 209.4 jit_solution(9867939885913287418)
XLA Ops:
  0.0 1.4 copy.13.weights
  1.4 1.5 copy.12.ids
  2.9 203.8 %layer.1 = bf16[192,4096]{1,0:T(8,128)(2,1)} custom-call(bf16[192,4096]{1,0:T(8,128)(2,1)} %tokens.1, s32[192,8]{1,0:T(8,128)} %copy.12.ids, bf16[192,8]{1,0:T(8,128)(2,1)} %copy.13.weights, f32[1,1024,1536]{2,1,0:T(8,128)} %mgu.1, bf16[1,1024,1536]{2,1,0:T(8,128)(2,1)} %ggu.1, bf16[1,1024,1536]{2,1,0:T(8,128)(2,1)} %fgu.1, bf16[1,1024,1536]{2,1,0:T(8,128)(2,1)} %vgu.1, ...), custom_call_target="tpu_custom_call" | custom-call | flops 16999999488 | bytes 30000000 | tf_op jit(solution)/shard_map/layer/pallas_call | solution.py:575
  206.7 2.7 %copy.15 = bf16[192,4096]{1,0:T(8,128)(2,1)} copy(bf16[192,4096]{1,0:T(8,128)(2,1)} %layer.1) | data formatting | bytes 3145728

commit v3 on v2

--- a/solution.py
+++ b/solution.py
@@ -116,7 +116,8 @@
 
     peers = []
     sources = []
-    for dx, dz in OFFSETS:
+    for ax, az in OFFSETS:
+        dx, dz = ax + (az - ax) * core, az + (ax - az) * core
         px, pz = (x + dx) % 4, (zz + dz) % 4
         qx, qz = (x + 4 - dx) % 4, (zz + 4 - dz) % 4
         peers.append((at(px, y, pz, core), px * 4 + pz))
@@ -159,12 +160,12 @@
         for copy in dn_loads(chunk):
             copy.start()
 
-    lane = lax.broadcasted_iota(jnp.int32, (TOK, 128), 1)
-    mine = jnp.zeros((TOK, 128), F32)
-    theirs = jnp.zeros((TOK, 128), F32)
+    lane = lax.broadcasted_iota(jnp.int32, (128, TOK), 0)
+    mine = jnp.zeros((128, TOK), F32)
+    theirs = jnp.zeros((128, TOK), F32)
     for k in range(8):
-        named = ids[:, k : k + 1]
-        weight = weights[:, k : k + 1].astype(F32)
+        named = ids[k : k + 1, :]
+        weight = weights[k : k + 1, :].astype(F32)
         for other in range(2):
             row = yl if other == 0 else 1 - yl
             value = jnp.where(
@@ -176,8 +177,8 @@
                 mine = mine + value
             else:
                 theirs = theirs + value
-    pk[0:TOK, :] = mine
-    pks[...] = theirs
+    pk[0:TOK, :] = jnp.transpose(mine)
+    pks[...] = jnp.transpose(theirs)
 
     barrier = pltpu.get_barrier_semaphore()
     greeted = [dev for dev, _ in peers] + [sib_dev, far_dev, to_dev, from_dev]
@@ -344,10 +345,10 @@
     lax.fori_loop(4, 6, adam_gu, 0)
     dispatch(2)
     lax.fori_loop(6, 8, adam_gu, 0)
+    send_gu(0)
     dispatch(3)
     scg_far = start(remote(scg.at[0], scg.at[2], sc_s.at[1], sc_r.at[1], far_dev))
     scg_sib = start(remote(scg.at[0], scg.at[1], sc_s.at[0], sc_r.at[0], sib_dev))
-    send_gu(0)
     send_gu(1)
     send_gu(2)
     send_gu(3)
@@ -483,13 +484,20 @@
 
         def column_tile(n, carry):
             cols = pl.ds(pl.multiple_of(n * 256, 256), 256)
-            both = jnp.dot(comb[...], ret[k, :, cols], preferred_element_type=F32)
-            acc[k * TOK : (k + 1) * TOK, cols] = both[:TOK]
-            ps[k, :, cols] = both[TOK:].astype(BF16)
+            other = jnp.dot(comb[TOK:, :], ret[k, :, cols], preferred_element_type=F32)
+            ps[k, :, cols] = other.astype(BF16)
+            return carry
+
+        def own_tile(n, carry):
+            cols = pl.ds(pl.multiple_of(n * 256, 256), 256)
+            acc[k * TOK : (k + 1) * TOK, cols] = jnp.dot(
+                comb[0:TOK, :], ret[k, :, cols], preferred_element_type=F32
+            )
             return carry
 
         lax.fori_loop(0, DC // 256, column_tile, 0)
         partial.append(start(remote(ps.at[k], pr.at[k], par_s.at[k], par_r.at[k], from_dev)))
+        lax.fori_loop(0, DC // 256, own_tile, 0)
 
     written = []
 
@@ -585,7 +593,7 @@
         cost_estimate=pl.CostEstimate(
             flops=17_000_000_000, bytes_accessed=30_000_000, transcendentals=5_000_000
         ),
-    )(*args)
+    )(args[0], args[1].T, args[2].T, *args[3:])
 
 
 def solution(mesh):

time: 210 us -> 196 us (0.933)
  Pallas kernels: 204 us -> 192 us
  local copies, waits for them, and re-layouts: 5.58 us -> 2.7 us
    pallas_call x1, Pallas kernels: 204 us -> 192 us  [shards(): pl.pallas_call(kernel, name='layer', out_shape=jax.ShapeDtypeStruct((TOK,...]
    unnamed x3 -> x1, local copies, waits for them, and re-layouts: 5.58 us -> 2.7 us
where the time goes in v3:
time: 196 us; the launch traced here: 195 us
  Pallas kernels  192 us (98%)
  local copies, waits for them, and re-layouts  2.7 us (1%)
    pallas_call x1, Pallas kernels, shards(): pl.pallas_call(kernel, name='layer', out_shape=jax.ShapeDtypeStruct((TOK,...  192 us

profile of v3, /device:TPU:8, one launch (start us, length us, event | category | flops | bytes accessed | tf_op | source)
XLA Modules:
  0.0 195.2 jit_solution(5919944222663640061)
XLA Ops:
  0.0 192.5 %layer.1 = bf16[192,4096]{1,0:T(8,128)(2,1)} custom-call(bf16[192,4096]{1,0:T(8,128)(2,1)} %tokens.1, s32[8,192]{1,0:T(8,128)} %bitcast.2, bf16[8,192]{1,0:T(8,128)(2,1)} %bitcast.3, f32[1,1024,1536]{2,1,0:T(8,128)} %mgu.1, bf16[1,1024,1536]{2,1,0:T(8,128)(2,1)} %ggu.1, bf16[1,1024,1536]{2,1,0:T(8,128)(2,1)} %fgu.1, bf16[1,1024,1536]{2,1,0:T(8,128)(2,1)} %vgu.1, ...), custom_call_target="tpu_custom_call" | custom-call | flops 16999999488 | bytes 30000000 | tf_op jit(solution)/shard_map/layer/pallas_call | solution.py:583
  192.5 2.7 %copy.13 = bf16[192,4096]{1,0:T(8,128)(2,1)} copy(bf16[192,4096]{1,0:T(8,128)(2,1)} %layer.1) | data formatting | bytes 3145728

commit v4 on v3

--- a/solution.py
+++ b/solution.py
@@ -20,8 +20,8 @@
 SHARD = 1024
 CHUNKS = 4
 DC = D // CHUNKS
-PARTS = 4
-PART = SHARD // PARTS
+PART_AT = (0, 256, 512, 896, 1024)
+PARTS = len(PART_AT) - 1
 
 beta_one = 0.9
 beta_two = 0.999
@@ -128,6 +128,11 @@
 
     def columns(zero_index, k):
         return pl.ds(pl.multiple_of(chunk_of(zero_index, k) * DC, DC), DC)
+
+    barrier = pltpu.get_barrier_semaphore()
+    greeted = [dev for dev, _ in peers] + [sib_dev, far_dev, to_dev, from_dev]
+    for dev in greeted:
+        pl.semaphore_signal(barrier, inc=1, device_id=dev, device_id_type=MESH)
 
     own_tok = []
     for k in range(CHUNKS):
@@ -180,10 +185,6 @@
     pk[0:TOK, :] = jnp.transpose(mine)
     pks[...] = jnp.transpose(theirs)
 
-    barrier = pltpu.get_barrier_semaphore()
-    greeted = [dev for dev, _ in peers] + [sib_dev, far_dev, to_dev, from_dev]
-    for dev in greeted:
-        pl.semaphore_signal(barrier, inc=1, device_id=dev, device_id_type=MESH)
     pl.semaphore_wait(barrier, len(greeted))
 
     sends = []
@@ -255,7 +256,7 @@
         return carry
 
     def part_rows(p):
-        return pl.ds(p * PART, PART)
+        return pl.ds(PART_AT[p], PART_AT[p + 1] - PART_AT[p])
 
     gu_sib, gu_far = [], []
 
@@ -305,7 +306,7 @@
     dispatched = [[] for _ in range(CHUNKS)]
     kept = []
 
-    def dispatch(k):
+    def dispatch(k, also=()):
         tok_copy[k].wait_recv()
 
         def column_tile(n, carry):
@@ -322,6 +323,9 @@
             )
             copy.start()
             dispatched[k].append(copy)
+            for p, after in also:
+                if after == i:
+                    send_gu(p)
         copy = pltpu.make_async_copy(og.at[k, slot_rows(pe)], xr.at[k, slot_rows(pe)], dis_l.at[k])
         copy.start()
         kept.append(copy)
@@ -346,10 +350,9 @@
     dispatch(2)
     lax.fori_loop(6, 8, adam_gu, 0)
     send_gu(0)
-    dispatch(3)
+    dispatch(3, ((1, 7),))
     scg_far = start(remote(scg.at[0], scg.at[2], sc_s.at[1], sc_r.at[1], far_dev))
     scg_sib = start(remote(scg.at[0], scg.at[1], sc_s.at[0], sc_r.at[0], sib_dev))
-    send_gu(1)
     send_gu(2)
     send_gu(3)
     lax.fori_loop(0, 8, adam_dn, 0)
@@ -412,17 +415,17 @@
     gated(2, range(4))
     forward_gu(2)
     send_dn(0)
-    gated(2, range(4, 6))
+    gated(2, range(4, 7))
     arrived(3)
     scg_fwd.wait_recv()
     for p in range(3):
         gu_fwd[p].wait_recv()
-    gated(3, range(6))
+    gated(3, range(7))
     forward_gu(3)
     send_dn(1)
-    gated(2, range(6, 8))
+    gated(2, range(7, 8))
     gu_fwd[3].wait_recv()
-    gated(3, range(6, 8))
+    gated(3, range(7, 8))
 
     def activate(n, carry):
         cols = pl.ds(pl.multiple_of(n * 256, 256), 256)
@@ -495,17 +498,29 @@
             )
             return carry
 
-        lax.fori_loop(0, DC // 256, column_tile, 0)
-        partial.append(start(remote(ps.at[k], pr.at[k], par_s.at[k], par_r.at[k], from_dev)))
+        halves = []
+        for h in range(2):
+            lax.fori_loop(2 * h, 2 * h + 2, column_tile, 0)
+            cols = pl.ds(h * 512, 512)
+            halves.append(
+                start(
+                    remote(
+                        ps.at[k, :, cols], pr.at[k, :, cols], par_s.at[k, h], par_r.at[k, h], from_dev
+                    )
+                )
+            )
+        partial.append(halves)
         lax.fori_loop(0, DC // 256, own_tile, 0)
 
     written = []
 
     def finish(k):
-        partial[k].wait_recv()
         here = k + 2 * apart * (1 - 2 * (k // 2))
         rows = pl.ds(pl.multiple_of(here * TOK, TOK), TOK)
-        tokv[k, 0:TOK, :] = (acc[rows, 0:DC] + pr[k].astype(F32)).astype(BF16)
+        for h in range(2):
+            partial[k][h].wait_recv()
+            cols = slice(h * 512, h * 512 + 512)
+            tokv[k, 0:TOK, cols] = (acc[rows, cols] + pr[k, :, cols].astype(F32)).astype(BF16)
         copy = pltpu.make_async_copy(
             tokv.at[k, pl.ds(0, TOK)], out.at[:, columns(zero_to, k)], out_sem.at[k]
         )
@@ -577,7 +592,7 @@
         dma((CHUNKS,)), dma((CHUNKS, PEERS)), dma((CHUNKS, PEERS)),
         dma((3, PARTS)), dma((3, PARTS)), dma((3, 2)), dma((3, 2)),
         dma((6,)), dma((6,)),
-        dma((CHUNKS,)), dma((CHUNKS,)),
+        dma((CHUNKS, 2)), dma((CHUNKS, 2)),
         dma((2, 4)), dma((2, 4)), dma((CHUNKS,)),
     ]
     return pl.pallas_call(

time: 196 us -> 193 us (0.985)
  Pallas kernels: 192 us -> 190 us
    pallas_call x1, Pallas kernels: 192 us -> 190 us  [shards(): pl.pallas_call(kernel, name='layer', out_shape=jax.ShapeDtypeStruct((TOK,...]
where the time goes in v4:
time: 193 us
  Pallas kernels  190 us (98%)
  local copies, waits for them, and re-layouts  2.7 us (1%)
    pallas_call x1, Pallas kernels, shards(): pl.pallas_call(kernel, name='layer', out_shape=jax.ShapeDtypeStruct((TOK,...  190 us

profile of v4, /device:TPU:8, one launch (start us, length us, event | category | flops | bytes accessed | tf_op | source)
XLA Modules:
  0.0 193.0 jit_solution(13855397976686149732)
XLA Ops:
  0.0 190.3 %layer.1 = bf16[192,4096]{1,0:T(8,128)(2,1)} custom-call(bf16[192,4096]{1,0:T(8,128)(2,1)} %tokens.1, s32[8,192]{1,0:T(8,128)} %bitcast.2, bf16[8,192]{1,0:T(8,128)(2,1)} %bitcast.3, f32[1,1024,1536]{2,1,0:T(8,128)} %mgu.1, bf16[1,1024,1536]{2,1,0:T(8,128)(2,1)} %ggu.1, bf16[1,1024,1536]{2,1,0:T(8,128)(2,1)} %fgu.1, bf16[1,1024,1536]{2,1,0:T(8,128)(2,1)} %vgu.1, ...), custom_call_target="tpu_custom_call" | custom-call | flops 16999999488 | bytes 30000000 | tf_op jit(solution)/shard_map/layer/pallas_call | solution.py:598
  190.3 2.7 %copy.13 = bf16[192,4096]{1,0:T(8,128)(2,1)} copy(bf16[192,4096]{1,0:T(8,128)(2,1)} %layer.1) | data formatting | bytes 3145728

commit v5 on v4

--- a/solution.py
+++ b/solution.py
@@ -457,33 +457,45 @@
             og[k, :, cols] = total.astype(BF16)
             return carry
 
-        lax.fori_loop(0, DC // 256, row_tile, 0)
-        for i, (dev, p) in enumerate(peers):
-            start(
+        pieces = 2 if k == CHUNKS - 1 else 1
+        local = []
+        for h in range(pieces):
+            tiles = DC // 256 // pieces
+            lax.fori_loop(h * tiles, (h + 1) * tiles, row_tile, 0)
+            cols = pl.ds(h * (DC // pieces), DC // pieces)
+            for i, (dev, p) in enumerate(peers):
+                start(
+                    remote(
+                        og.at[k, slot_rows(p), cols],
+                        ret.at[k, slot_rows(pe), cols],
+                        ret_s.at[k + h, i],
+                        ret_r.at[k + h, i],
+                        dev,
+                    )
+                )
+            copy = pltpu.make_async_copy(
+                og.at[k, slot_rows(pe), cols], ret.at[k, slot_rows(pe), cols], ret_l.at[k + h]
+            )
+            copy.start()
+            local.append(copy)
+        returned.append(local)
+
+    partial = []
+
+    def mix(k):
+        pieces = len(returned[k])
+
+        def returns_in(h):
+            returned[k][h].wait()
+            cols = pl.ds(h * (DC // pieces), DC // pieces)
+            for i, p in enumerate(sources):
                 remote(
-                    og.at[k, slot_rows(p)],
-                    ret.at[k, slot_rows(pe)],
-                    ret_s.at[k, i],
-                    ret_r.at[k, i],
-                    dev,
-                )
-            )
-        copy = pltpu.make_async_copy(og.at[k, slot_rows(pe)], ret.at[k, slot_rows(pe)], ret_l.at[k])
-        copy.start()
-        returned.append(copy)
-
-    partial = []
-
-    def mix(k):
-        returned[k].wait()
-        for i, p in enumerate(sources):
-            remote(
-                og.at[k, slot_rows(p)],
-                ret.at[k, slot_rows(p)],
-                ret_s.at[k, i],
-                ret_r.at[k, i],
-                peers[i][0],
-            ).wait_recv()
+                    og.at[k, slot_rows(p), cols],
+                    ret.at[k, slot_rows(p), cols],
+                    ret_s.at[k + h, i],
+                    ret_r.at[k + h, i],
+                    peers[i][0],
+                ).wait_recv()
 
         def column_tile(n, carry):
             cols = pl.ds(pl.multiple_of(n * 256, 256), 256)
@@ -500,6 +512,8 @@
 
         halves = []
         for h in range(2):
+            if h < pieces:
+                returns_in(h)
             lax.fori_loop(2 * h, 2 * h + 2, column_tile, 0)
             cols = pl.ds(h * 512, 512)
             halves.append(
@@ -589,7 +603,7 @@
         dma((CHUNKS,)), dma((CHUNKS,)), dma((CHUNKS,)),
         dma, dma,
         dma((CHUNKS,)), dma((CHUNKS, PEERS)), dma((CHUNKS, PEERS)),
-        dma((CHUNKS,)), dma((CHUNKS, PEERS)), dma((CHUNKS, PEERS)),
+        dma((CHUNKS + 1,)), dma((CHUNKS + 1, PEERS)), dma((CHUNKS + 1, PEERS)),
         dma((3, PARTS)), dma((3, PARTS)), dma((3, 2)), dma((3, 2)),
         dma((6,)), dma((6,)),
         dma((CHUNKS, 2)), dma((CHUNKS, 2)),

time: 193 us -> 191 us (0.990)
  Pallas kernels: 190 us -> 188 us
where the time goes in v5:
time: 191 us
  Pallas kernels  188 us (98%)
  local copies, waits for them, and re-layouts  2.7 us (1%)
    pallas_call x1, Pallas kernels, shards(): pl.pallas_call(kernel, name='layer', out_shape=jax.ShapeDtypeStruct((TOK,...  188 us

profile of v5, /device:TPU:8, one launch (start us, length us, event | category | flops | bytes accessed | tf_op | source)
XLA Modules:
  0.0 191.2 jit_solution(3279699888975028468)
XLA Ops:
  0.0 188.5 %layer.1 = bf16[192,4096]{1,0:T(8,128)(2,1)} custom-call(bf16[192,4096]{1,0:T(8,128)(2,1)} %tokens.1, s32[8,192]{1,0:T(8,128)} %bitcast.2, bf16[8,192]{1,0:T(8,128)(2,1)} %bitcast.3, f32[1,1024,1536]{2,1,0:T(8,128)} %mgu.1, bf16[1,1024,1536]{2,1,0:T(8,128)(2,1)} %ggu.1, bf16[1,1024,1536]{2,1,0:T(8,128)(2,1)} %fgu.1, bf16[1,1024,1536]{2,1,0:T(8,128)(2,1)} %vgu.1, ...), custom_call_target="tpu_custom_call" | custom-call | flops 16999999488 | bytes 30000000 | tf_op jit(solution)/shard_map/layer/pallas_call | solution.py:612
  188.5 2.7 %copy.13 = bf16[192,4096]{1,0:T(8,128)(2,1)} copy(bf16[192,4096]{1,0:T(8,128)(2,1)} %layer.1) | data formatting | bytes 3145728
